TPU v7x, 128 devices: a whole 4x4x4 slice. The times are simulated.
128 devices in a mesh: au: 16 (over x, y), vert: 8 (over z, core).
Axes of the slice: x: 4, y: 4, z: 4, core: 2. Of those that a mesh axis runs over, the one named last changes fastest.
Arguments:
- visibility: bfloat16 [262144, 128], P(('au', 'vert')), may hold values from -6 to 6
- destination: int32 [262144, 1], P(('au', 'vert')), may hold values from 0 to 127; in each aligned block of 2048 rows (0 to 2047, 2048 to 4095, ...) at most 32 rows name the same one
- cell_u: int32 [262144], P(('au', 'vert')), may hold values from 0 to 127
- cell_v: int32 [262144], P(('au', 'vert')), may hold values from 0 to 127
- tap_u: int32 [262144], P(('au', 'vert')), may hold values from 0 to 127
- tap_v: int32 [262144], P(('au', 'vert')), may hold values from 0 to 127
- kernel_table: bfloat16 [128, 8], replicated, may hold values from 0.19921875 to 1
Outputs:
- uv_grid: float32 [2048, 1024, 128], P('au', 'vert')
Inputs may be any that keep to these rules, and one draw needn't show every extreme that they name: `destination`: of the 2048 rows of one device, at most 32 name the same tile, and in every draw some device sends exactly 32 rows to some tile.
All inputs are finite; a program needn't handle non-finite values.
Results may differ from a plain program's by a relative error of at most 0.0029.
Values may be sent and summed in bfloat16 or wider, within the bound.
No kernel may reach another device: no remote copies, remote signals or barrier semaphores. Data moves between devices by JAX's collectives and lax.ppermute only.
A program may use at most 128 MiB of HBM per device.

v0:
```python
import math

import jax
import jax.numpy as jnp
from jax import lax
from jax.sharding import PartitionSpec as P

TU = 128
TV = 128


def padded(shard, sides, width):
    for axis, dim in sides:
        size, length = (lax.axis_size(axis), shard.shape[dim])
        up = [(i, (i + 1) % size) for i in range(size - 1)]
        down = [(j, i) for i, j in up]
        last = lax.slice_in_dim(shard, length - width, length, axis=dim)
        first = lax.slice_in_dim(shard, 0, width, axis=dim)
        before = lax.ppermute(last, axis, up)
        after = lax.ppermute(first, axis, down)
        shard = jnp.concatenate([before, shard, after], axis=dim)
    return shard


def spread_taps(offset, weights, extent):
    position = jnp.arange(extent, dtype=jnp.int32)[None, :]
    total = jnp.zeros((offset.shape[0], extent), jnp.float32)
    for tap in range(weights.shape[1]):
        total = total + jnp.where(position == offset[:, None] + tap, weights[:, tap : tap + 1], 0.0)
    return total


def local(visibility, destination, cell_u, cell_v, tap_u, tap_v, kernel_table):
    rows_here, feat = visibility.shape
    phases = kernel_table.shape[0]
    n_au = lax.axis_size("au")
    n_vert = lax.axis_size("vert")
    devices = n_au * n_vert
    capacity = 2 * rows_here // devices
    dest = destination[:, 0]
    onehot = (dest[:, None] == jnp.arange(devices, dtype=jnp.int32)[None, :]).astype(jnp.int32)
    ranks = jnp.sum(onehot * (jnp.cumsum(onehot, 0) - 1), 1)
    slot = dest * capacity + ranks
    placing = jnp.stack([cell_u, cell_v, tap_u, tap_v], 1)
    sent_vis = jnp.zeros((devices * capacity, feat), jnp.bfloat16).at[slot].set(visibility)
    sent_meta = jnp.zeros((devices * capacity, 4), jnp.int32).at[slot].set(placing)
    arrived = (
        lax.all_to_all(
            sent_vis.reshape(devices, capacity, feat),
            ("au", "vert"),
            split_axis=0,
            concat_axis=0,
            tiled=True,
        ),
        lax.all_to_all(
            sent_meta.reshape(devices, capacity, 4),
            ("au", "vert"),
            split_axis=0,
            concat_axis=0,
            tiled=True,
        ),
    )
    rows_vis = arrived[0].reshape(devices * capacity, feat)
    rows_meta = arrived[1].reshape(devices * capacity, 4)
    slots = devices * capacity
    block = math.gcd(slots, 512)
    ext_u = TU + 8
    ext_v = TV + 8
    phase_ids = jnp.arange(phases, dtype=jnp.int32)[None, :]

    def one_block(step, grid):
        vis = lax.dynamic_slice_in_dim(rows_vis, step * block, block, 0)
        meta = lax.dynamic_slice_in_dim(rows_meta, step * block, block, 0)
        pick_u = (meta[:, 2:3] == phase_ids).astype(jnp.bfloat16)
        pick_v = (meta[:, 3:4] == phase_ids).astype(jnp.bfloat16)
        ku = jnp.dot(pick_u, kernel_table, preferred_element_type=jnp.float32)
        kv = jnp.dot(pick_v, kernel_table, preferred_element_type=jnp.float32)
        weight_u = spread_taps(meta[:, 0], ku, ext_u).astype(jnp.bfloat16)
        weight_v = spread_taps(meta[:, 1], kv, ext_v)
        weighted = (weight_v[:, :, None] * vis.astype(jnp.float32)[:, None, :]).astype(jnp.bfloat16)
        weighted = weighted.reshape(block, ext_v * feat)
        return grid + lax.dot_general(
            weight_u, weighted, (((0,), (0,)), ((), ())), preferred_element_type=jnp.float32
        )

    grid = lax.fori_loop(
        0, slots // block, one_block, jnp.zeros((ext_u, ext_v * feat), jnp.float32)
    )
    grid = grid.reshape(ext_u, ext_v, feat)
    edges_u = jnp.concatenate([grid[0:4], grid[TU + 4 : TU + 8]], 0)
    around_u = padded(edges_u, (("au", 0),), 4)
    middle = grid[4 : TU + 4]
    middle = middle.at[0:4].add(around_u[0:4])
    middle = middle.at[TU - 4 : TU].add(around_u[12:16])
    edges_v = jnp.concatenate([middle[:, 0:4], middle[:, TV + 4 : TV + 8]], 1)
    around_v = padded(edges_v, (("vert", 1),), 4)
    inner = middle[:, 4 : TV + 4]
    inner = inner.at[:, 0:4].add(around_v[:, 0:4])
    inner = inner.at[:, TV - 4 : TV].add(around_v[:, 12:16])
    return inner


def solution(mesh):
    return jax.shard_map(
        local,
        mesh=mesh,
        in_specs=(
            P(("au", "vert"), None),
            P(("au", "vert"), None),
            P(("au", "vert")),
            P(("au", "vert")),
            P(("au", "vert")),
            P(("au", "vert")),
            P(),
        ),
        out_specs=P("au", "vert", None),
        check_vma=False,
    )
```

profile of v0, /device:TPU:1, one launch (start us, length us, event | category | flops | bytes accessed | tf_op | source)
XLA Modules:
  0.0 338.5 jit_solution(6002760609826377652)
XLA Ops:
  0.0 0.8 copy.16
  1.6 1.3 fusion.26
  3.7 0.8 pad_add_fusion
  4.8 6.1 %scatter_custom_fusion = s32[4096,4]{1,0:T(8,128)S(1)} fusion(s32[2048]{0:T(1024)S(1)} %bitcast.205, s32[2048,4]{1,0:T(8,128)S(1)} %copy.18, s32[]{:T(128)} %constant.188.clone.1), kind=kCustom, calls=%fused_computation.73 | custom fusion | bytes 65540 | tf_op jit(solution)/shard_map/scatter | solution.py:46
  10.9 0.8 copy.20
  11.8 0.8 reshape.544
  12.6 11.5 %all-to-all-start = ((s32[128,1,128]{2,1,0:T(1,128)}), s32[128,1,128]{2,1,0:T(1,128)S(1)}, u32[]{:S(2)}, u32[]{:S(2)}) async-start(s32[128,1,128]{2,1,0:T(1,128)} %reshape.544), calls=%async_computation | async-start | bytes 131072 | tf_op jit(solution)/shard_map/all_to_all | solution.py:55
  24.1 7.1 %scatter_custom_fusion.1 = bf16[4096,128]{1,0:T(8,128)(2,1)} fusion(s32[2048]{0:T(1024)S(1)} %bitcast.206, bf16[2048,128]{1,0:T(8,128)(2,1)} %param.17, bf16[]{:T(256)} %constant.190.clone.1), kind=kCustom, calls=%fused_computation.75 | custom fusion | bytes 1049088 | tf_op jit(solution)/shard_map/scatter | solution.py:45
  31.3 2.2 all-to-all-done
  33.5 7.6 %all-to-all-start.1 = ((bf16[128,32,128]{2,1,0:T(8,128)(2,1)}), bf16[128,32,128]{2,1,0:T(8,128)(2,1)S(1)}, u32[]{:S(2)}, u32[]{:S(2)}) async-start(bf16[128,32,128]{2,1,0:T(8,128)(2,1)} %bitcast.12), calls=%async_computation.1 | async-start | bytes 2097152 | tf_op jit(solution)/shard_map/all_to_all | solution.py:48
  41.6 0.8 reduce.8
  42.7 17.6 %all-to-all-done.1 = bf16[128,32,128]{2,1,0:T(8,128)(2,1)S(1)} async-done(((bf16[128,32,128]{2,1,0:T(8,128)(2,1)}), bf16[128,32,128]{2,1,0:T(8,128)(2,1)S(1)}, u32[]{:S(2)}, u32[]{:S(2)}) %all-to-all-start.1) | async-done | bytes 1048608 | tf_op jit(solution)/shard_map/all_to_all | solution.py:48
  60.3 252.6 %while.19 = (s32[]{:T(128)}, f32[136,17408]{1,0:T(8,128)}, s32[4096,4]{0,1:T(4,128)S(1)}, bf16[128,8]{0,1:T(8,128)(2,1)S(1)}, bf16[4096,128]{1,0:T(8,128)(2,1)S(...) while((s32[]{:T(128)}, f32[136,17408]{1,0:T(8,128)}, ...), condition=%wide.region_6.7_spmd.clone.clone, body=%wide.region_5.6_spmd.clone.clone.sunk | while | flops 2452442112 | bytes 56025324 | solution.py:86
  61.0 1.1 select_add_fusion.2
  62.2 12.9 %multiply_convert_fusion.2 = bf16[512,136,128]{2,1,0:T(8,128)(2,1)} fusion(f32[512,128]{1,0:T(8,128)S(1)} %dynamic-slice_convert_fusion.2, f32[512,136]{1,0:T(8,128)S(1)} %select_add_fusion.2), kind=kLoop, calls=%fused_computation.3.clone.1 | loop fusion | flops 17825792 | bytes 18366464 | tf_op jit(solution)/shard_map/while/body/eval_jaxpr/convert_element_type | solution.py:80
  75.1 14.4 %convolution_add_fusion.2 = f32[136,17408]{1,0:T(8,128)} fusion(bf16[64,8,136,128]{3,2,1,0:T(8,128)(2,1)} %bitcast.160, f32[136,17408]{1,0:T(8,128)} %get-tuple-element.371, pred[]{:T(512)S(6)} %compare.25, f32[512]{0:T(512)S(1)} %bitcast.172, s32[512]{0:T(512)S(1)} %bitcast.165, f32[512]{0:T(512)S(1)} %bitcast.173, s32[512]{0:T(512)S(1)} %bitcast.169, ...), kind=kOutput, calls=%fused_computation.4.clone.1 | convolution fusion | flops 2430713856 | bytes 36798464 | tf_op jit(solution)/shard_map/while/body/eval_jaxpr/dot_general | solution.py:82
  90.2 1.1 select_add_fusion.2
  91.4 12.9 %multiply_convert_fusion.2 = bf16[512,136,128]{2,1,0:T(8,128)(2,1)} fusion(f32[512,128]{1,0:T(8,128)S(1)} %dynamic-slice_convert_fusion.2, f32[512,136]{1,0:T(8,128)S(1)} %select_add_fusion.2), kind=kLoop, calls=%fused_computation.3.clone.1 | loop fusion | flops 17825792 | bytes 18366464 | tf_op jit(solution)/shard_map/while/body/eval_jaxpr/convert_element_type | solution.py:80
  104.3 17.1 %convolution_add_fusion.2 = f32[136,17408]{1,0:T(8,128)} fusion(bf16[64,8,136,128]{3,2,1,0:T(8,128)(2,1)} %bitcast.160, f32[136,17408]{1,0:T(8,128)} %get-tuple-element.371, pred[]{:T(512)S(6)} %compare.25, f32[512]{0:T(512)S(1)} %bitcast.172, s32[512]{0:T(512)S(1)} %bitcast.165, f32[512]{0:T(512)S(1)} %bitcast.173, s32[512]{0:T(512)S(1)} %bitcast.169, ...), kind=kOutput, calls=%fused_computation.4.clone.1 | convolution fusion | flops 2430713856 | bytes 36798464 | tf_op jit(solution)/shard_map/while/body/eval_jaxpr/dot_general | solution.py:82
  122.1 1.1 select_add_fusion.2
  123.3 12.9 %multiply_convert_fusion.2 = bf16[512,136,128]{2,1,0:T(8,128)(2,1)} fusion(f32[512,128]{1,0:T(8,128)S(1)} %dynamic-slice_convert_fusion.2, f32[512,136]{1,0:T(8,128)S(1)} %select_add_fusion.2), kind=kLoop, calls=%fused_computation.3.clone.1 | loop fusion | flops 17825792 | bytes 18366464 | tf_op jit(solution)/shard_map/while/body/eval_jaxpr/convert_element_type | solution.py:80
  136.2 17.1 %convolution_add_fusion.2 = f32[136,17408]{1,0:T(8,128)} fusion(bf16[64,8,136,128]{3,2,1,0:T(8,128)(2,1)} %bitcast.160, f32[136,17408]{1,0:T(8,128)} %get-tuple-element.371, pred[]{:T(512)S(6)} %compare.25, f32[512]{0:T(512)S(1)} %bitcast.172, s32[512]{0:T(512)S(1)} %bitcast.165, f32[512]{0:T(512)S(1)} %bitcast.173, s32[512]{0:T(512)S(1)} %bitcast.169, ...), kind=kOutput, calls=%fused_computation.4.clone.1 | convolution fusion | flops 2430713856 | bytes 36798464 | tf_op jit(solution)/shard_map/while/body/eval_jaxpr/dot_general | solution.py:82
  154.0 1.1 select_add_fusion.2
  155.2 12.9 %multiply_convert_fusion.2 = bf16[512,136,128]{2,1,0:T(8,128)(2,1)} fusion(f32[512,128]{1,0:T(8,128)S(1)} %dynamic-slice_convert_fusion.2, f32[512,136]{1,0:T(8,128)S(1)} %select_add_fusion.2), kind=kLoop, calls=%fused_computation.3.clone.1 | loop fusion | flops 17825792 | bytes 18366464 | tf_op jit(solution)/shard_map/while/body/eval_jaxpr/convert_element_type | solution.py:80
  168.1 17.1 %convolution_add_fusion.2 = f32[136,17408]{1,0:T(8,128)} fusion(bf16[64,8,136,128]{3,2,1,0:T(8,128)(2,1)} %bitcast.160, f32[136,17408]{1,0:T(8,128)} %get-tuple-element.371, pred[]{:T(512)S(6)} %compare.25, f32[512]{0:T(512)S(1)} %bitcast.172, s32[512]{0:T(512)S(1)} %bitcast.165, f32[512]{0:T(512)S(1)} %bitcast.173, s32[512]{0:T(512)S(1)} %bitcast.169, ...), kind=kOutput, calls=%fused_computation.4.clone.1 | convolution fusion | flops 2430713856 | bytes 36798464 | tf_op jit(solution)/shard_map/while/body/eval_jaxpr/dot_general | solution.py:82
  186.0 1.1 select_add_fusion.2
  187.1 12.9 %multiply_convert_fusion.2 = bf16[512,136,128]{2,1,0:T(8,128)(2,1)} fusion(f32[512,128]{1,0:T(8,128)S(1)} %dynamic-slice_convert_fusion.2, f32[512,136]{1,0:T(8,128)S(1)} %select_add_fusion.2), kind=kLoop, calls=%fused_computation.3.clone.1 | loop fusion | flops 17825792 | bytes 18366464 | tf_op jit(solution)/shard_map/while/body/eval_jaxpr/convert_element_type | solution.py:80
  200.0 17.1 %convolution_add_fusion.2 = f32[136,17408]{1,0:T(8,128)} fusion(bf16[64,8,136,128]{3,2,1,0:T(8,128)(2,1)} %bitcast.160, f32[136,17408]{1,0:T(8,128)} %get-tuple-element.371, pred[]{:T(512)S(6)} %compare.25, f32[512]{0:T(512)S(1)} %bitcast.172, s32[512]{0:T(512)S(1)} %bitcast.165, f32[512]{0:T(512)S(1)} %bitcast.173, s32[512]{0:T(512)S(1)} %bitcast.169, ...), kind=kOutput, calls=%fused_computation.4.clone.1 | convolution fusion | flops 2430713856 | bytes 36798464 | tf_op jit(solution)/shard_map/while/body/eval_jaxpr/dot_general | solution.py:82
  217.9 1.1 select_add_fusion.2
  219.0 12.9 %multiply_convert_fusion.2 = bf16[512,136,128]{2,1,0:T(8,128)(2,1)} fusion(f32[512,128]{1,0:T(8,128)S(1)} %dynamic-slice_convert_fusion.2, f32[512,136]{1,0:T(8,128)S(1)} %select_add_fusion.2), kind=kLoop, calls=%fused_computation.3.clone.1 | loop fusion | flops 17825792 | bytes 18366464 | tf_op jit(solution)/shard_map/while/body/eval_jaxpr/convert_element_type | solution.py:80
  231.9 17.1 %convolution_add_fusion.2 = f32[136,17408]{1,0:T(8,128)} fusion(bf16[64,8,136,128]{3,2,1,0:T(8,128)(2,1)} %bitcast.160, f32[136,17408]{1,0:T(8,128)} %get-tuple-element.371, pred[]{:T(512)S(6)} %compare.25, f32[512]{0:T(512)S(1)} %bitcast.172, s32[512]{0:T(512)S(1)} %bitcast.165, f32[512]{0:T(512)S(1)} %bitcast.173, s32[512]{0:T(512)S(1)} %bitcast.169, ...), kind=kOutput, calls=%fused_computation.4.clone.1 | convolution fusion | flops 2430713856 | bytes 36798464 | tf_op jit(solution)/shard_map/while/body/eval_jaxpr/dot_general | solution.py:82
  249.8 1.1 select_add_fusion.2
  250.9 12.9 %multiply_convert_fusion.2 = bf16[512,136,128]{2,1,0:T(8,128)(2,1)} fusion(f32[512,128]{1,0:T(8,128)S(1)} %dynamic-slice_convert_fusion.2, f32[512,136]{1,0:T(8,128)S(1)} %select_add_fusion.2), kind=kLoop, calls=%fused_computation.3.clone.1 | loop fusion | flops 17825792 | bytes 18366464 | tf_op jit(solution)/shard_map/while/body/eval_jaxpr/convert_element_type | solution.py:80
  263.9 17.1 %convolution_add_fusion.2 = f32[136,17408]{1,0:T(8,128)} fusion(bf16[64,8,136,128]{3,2,1,0:T(8,128)(2,1)} %bitcast.160, f32[136,17408]{1,0:T(8,128)} %get-tuple-element.371, pred[]{:T(512)S(6)} %compare.25, f32[512]{0:T(512)S(1)} %bitcast.172, s32[512]{0:T(512)S(1)} %bitcast.165, f32[512]{0:T(512)S(1)} %bitcast.173, s32[512]{0:T(512)S(1)} %bitcast.169, ...), kind=kOutput, calls=%fused_computation.4.clone.1 | convolution fusion | flops 2430713856 | bytes 36798464 | tf_op jit(solution)/shard_map/while/body/eval_jaxpr/dot_general | solution.py:82
  281.7 1.1 select_add_fusion.2
  282.8 12.9 %multiply_convert_fusion.2 = bf16[512,136,128]{2,1,0:T(8,128)(2,1)} fusion(f32[512,128]{1,0:T(8,128)S(1)} %dynamic-slice_convert_fusion.2, f32[512,136]{1,0:T(8,128)S(1)} %select_add_fusion.2), kind=kLoop, calls=%fused_computation.3.clone.1 | loop fusion | flops 17825792 | bytes 18366464 | tf_op jit(solution)/shard_map/while/body/eval_jaxpr/convert_element_type | solution.py:80
  295.8 17.1 %convolution_add_fusion.2 = f32[136,17408]{1,0:T(8,128)} fusion(bf16[64,8,136,128]{3,2,1,0:T(8,128)(2,1)} %bitcast.160, f32[136,17408]{1,0:T(8,128)} %get-tuple-element.371, pred[]{:T(512)S(6)} %compare.25, f32[512]{0:T(512)S(1)} %bitcast.172, s32[512]{0:T(512)S(1)} %bitcast.165, f32[512]{0:T(512)S(1)} %bitcast.173, s32[512]{0:T(512)S(1)} %bitcast.169, ...), kind=kOutput, calls=%fused_computation.4.clone.1 | convolution fusion | flops 2430713856 | bytes 36798464 | tf_op jit(solution)/shard_map/while/body/eval_jaxpr/dot_general | solution.py:82
  312.9 1.5 slice_bitcast_fusion.1
  314.5 2.1 collective-permute-start
  316.6 1.3 collective-permute-start.1
  317.9 4.5 %slice_bitcast_fusion = f32[16,8,136,128]{3,1,2,0:T(8,128)S(1)} fusion(f32[136,17408]{1,0:T(8,128)} %get-tuple-element.165), kind=kLoop, calls=%fused_computation.65 | loop fusion | bytes 17825792
  322.4 1.5 copy.25
  324.0 1.1 collective-permute-done.1
  325.3 3.7 %collective-permute-start.2 = (f32[128,4,128]{2,1,0:T(4,128)S(1)}, f32[128,4,128]{2,1,0:T(4,128)S(1)}, u32[]{:S(2)}, u32[]{:S(2)}) collective-permute-start(f32[128,4,128]{2,1,0:T(4,128)S(1)} %get-tuple-element.258), channel_id=1, source_target_pairs={{0,1},{1,2},{2,3},{3,4},{4,5},{5,6},{6,7},{8,9},{9,10},{10,11},{11... | collective-permute-start | bytes 786440 | tf_op jit(solution)/shard_map/ppermute | solution.py:19
  329.0 2.0 collective-permute-start.3
  331.0 1.3 slice.382
  332.5 4.2 %collective-permute-done.3 = f32[128,4,128]{2,1,0:T(4,128)S(1)} collective-permute-done((f32[128,4,128]{2,1,0:T(4,128)S(1)}, f32[128,4,128]{2,1,0:T(4,128)S(1)}, u32[]{:S(2)}, u32[]{:S(2)}) %collective-permute-start.3) | collective-permute-done | bytes 262176 | tf_op jit(solution)/shard_map/ppermute | solution.py:20
  336.7 1.8 fusion.36
  (81 shorter events, 8.5 us)
Async XLA Ops:
  0.0 60.3 %copy-start.1 = (bf16[128,8]{0,1:T(8,128)(2,1)S(1)}, bf16[128,8]{0,1:T(8,128)(2,1)}, u32[]{:S(2)}) copy-start(bf16[128,8]{0,1:T(8,128)(2,1)} %param.23) | copy-start | bytes 6148
  12.6 20.9 %all-to-all-start = ((s32[128,1,128]{2,1,0:T(1,128)}), s32[128,1,128]{2,1,0:T(1,128)S(1)}, u32[]{:S(2)}, u32[]{:S(2)}) async-start(s32[128,1,128]{2,1,0:T(1,128)} %reshape.544), calls=%async_computation | async-start | bytes 131072 | tf_op jit(solution)/shard_map/all_to_all | solution.py:55
  33.5 26.8 %all-to-all-start.1 = ((bf16[128,32,128]{2,1,0:T(8,128)(2,1)}), bf16[128,32,128]{2,1,0:T(8,128)(2,1)S(1)}, u32[]{:S(2)}, u32[]{:S(2)}) async-start(bf16[128,32,128]{2,1,0:T(8,128)(2,1)} %bitcast.12), calls=%async_computation.1 | async-start | bytes 2097152 | tf_op jit(solution)/shard_map/all_to_all | solution.py:48
  314.5 9.4 %collective-permute-start = (f32[4,136,128]{2,1,0:T(8,128)S(1)}, f32[4,136,128]{2,1,0:T(8,128)S(1)}, u32[]{:S(2)}, u32[]{:S(2)}) collective-permute-start(f32[4,136,128]{2,1,0:T(8,128)S(1)} %bitcast.184), channel_id=1, source_target_pairs={{0,8},{8,16},{16,24},{24,32},{32,40},{40,48},{48,56},{56,64},{64,7... | collective-permute-start | bytes 835592 | tf_op jit(solution)/shard_map/ppermute | solution.py:19
  316.6 8.5 %collective-permute-start.1 = (f32[4,136,128]{2,1,0:T(8,128)S(1)}, f32[4,136,128]{2,1,0:T(8,128)S(1)}, u32[]{:S(2)}, u32[]{:S(2)}) collective-permute-start(f32[4,136,128]{2,1,0:T(8,128)S(1)} %bitcast.183), channel_id=1, source_target_pairs={{8,0},{16,8},{24,16},{32,24},{40,32},{48,40},{56,48},{64,56},{72,6... | collective-permute-start | bytes 835592 | tf_op jit(solution)/shard_map/ppermute | solution.py:20
  325.3 7.0 %collective-permute-start.2 = (f32[128,4,128]{2,1,0:T(4,128)S(1)}, f32[128,4,128]{2,1,0:T(4,128)S(1)}, u32[]{:S(2)}, u32[]{:S(2)}) collective-permute-start(f32[128,4,128]{2,1,0:T(4,128)S(1)} %get-tuple-element.258), channel_id=1, source_target_pairs={{0,1},{1,2},{2,3},{3,4},{4,5},{5,6},{6,7},{8,9},{9,10},{10,11},{11... | collective-permute-start | bytes 786440 | tf_op jit(solution)/shard_map/ppermute | solution.py:19
  329.0 7.7 %collective-permute-start.3 = (f32[128,4,128]{2,1,0:T(4,128)S(1)}, f32[128,4,128]{2,1,0:T(4,128)S(1)}, u32[]{:S(2)}, u32[]{:S(2)}) collective-permute-start(f32[128,4,128]{2,1,0:T(4,128)S(1)} %get-tuple-element.257), channel_id=1, source_target_pairs={{1,0},{2,1},{3,2},{4,3},{5,4},{6,5},{7,6},{9,8},{10,9},{11,10},{12... | collective-permute-start | bytes 786440 | tf_op jit(solution)/shard_map/ppermute | solution.py:20
  332.5 4.2 %copy-start = (f32[128,128,128]{2,1,0:T(8,128)}, f32[128,128,128]{2,1,0:T(8,128)S(1)}, u32[]{:S(2)}) copy-start(f32[128,128,128]{2,1,0:T(8,128)S(1)} %fusion.37) | copy-start | bytes 25165828
where the time goes:
time: 340 us; the launch traced here: 339 us
  matrix products  138 us (41%)
  other arithmetic  120 us (35%)
  starting transfers between devices  28.1 us (8%)
  local copies, waits for them, and re-layouts  26.6 us (8%)
  waiting for transfers between devices  25.2 us (7%)
    dot_general x8, matrix products, one_block(): lax.dot_general(weight_u, weighted, (((0,), (0,)), ((), ())), preferred_e...  134 us
    convert_element_type x8, other arithmetic, one_block(): (weight_v[:, :, None] * vis.astype(jnp.float32)[:, None, :]).astype(jnp.b...  103 us
    all_to_all x1, waiting for transfers between devices, local(): lax.all_to_all(sent_vis.reshape(devices, capacity, feat), ('au', 'vert'),...  17.6 us
    all_to_all x1, starting transfers between devices, local(): lax.all_to_all(sent_meta.reshape(devices, capacity, 4), ('au', 'vert'), s...  11.5 us
    add x8, other arithmetic, spread_taps(): total + jnp.where(position == offset[:, None] + tap, weights[:, tap:tap +...  9.18 us
    unnamed x11, local copies, waits for them, and re-layouts  8.59 us
    all_to_all x1, starting transfers between devices, local(): lax.all_to_all(sent_vis.reshape(devices, capacity, feat), ('au', 'vert'),...  7.56 us
    scatter x1, local copies, waits for them, and re-layouts, local(): jnp.zeros((devices * capacity, feat), jnp.bfloat16).at[slot].set(visibility)  7.14 us
  transfers between devices with their start and end apart: 6, of which 4 were waited for; matrix products, arithmetic and copies ran while one was open for 5% of the time, Pallas kernels for 0%

commit v1 on v0

v1 whole, which is shorter than its diff:
```python
import jax
import jax.numpy as jnp
from jax import lax
from jax.experimental import pallas as pl
from jax.experimental.pallas import tpu as pltpu
from jax.sharding import PartitionSpec as P

FEAT = 128
TAPS = 8
TU = 128
TV = 128
CAP = 32
SENT = CAP + 8
BLK = 256
EU = 144
EV = 144
PAD = 4
GROUP = 4
VMEM_LIMIT = 56 * 1024 * 1024
NT = (((1,), (1,)), ((), ()))

f32 = jnp.float32
bf16 = jnp.bfloat16
i32 = jnp.int32


def iota(shape, dim):
    return lax.broadcasted_iota(i32, shape, dim)


def dot(a, b):
    return jnp.dot(a, b, preferred_element_type=f32)


def earlier(n):
    return (iota((n, n), 0) < iota((n, n), 1)).astype(f32).astype(bf16)


def pack_kernel(dest_ref, cu_ref, cv_ref, tu_ref, tv_ref, vis_ref, out_ref, slot_v, slot_s, xf, packed, meta, sem):
    rows = vis_ref.shape[0]
    tiles = out_ref.shape[0]
    blocks = rows // BLK
    before = earlier(BLK)
    base = jnp.zeros((tiles, 1), f32)
    placed = jnp.zeros((tiles, 4 * CAP), f32)
    tile_ids = iota((tiles, BLK), 0)
    cap_ids = iota((CAP, BLK), 0)
    for b in range(blocks):
        part = pl.ds(b * BLK, BLK)
        d = dest_ref[:, part]
        mine = (tile_ids == d).astype(f32)
        mine16 = mine.astype(bf16)
        rank = jnp.sum(mine * (dot(mine16, before) + base), 0, keepdims=True).astype(i32)
        base = base + jnp.sum(mine, 1, keepdims=True)
        slot_v[pl.ds(b, 1), :] = d * CAP + rank
        at = cap_ids == rank
        fields = [
            jnp.where(at, (ref[:, part] + 1).astype(f32), 0.0)
            for ref in (cu_ref, cv_ref, tu_ref, tv_ref)
        ]
        fields = jnp.concatenate(fields, 0).astype(bf16)
        placed = placed + lax.dot_general(mine16, fields, NT, preferred_element_type=f32)
    meta[...] = placed
    copy = pltpu.make_async_copy(slot_v, slot_s, sem)
    copy.start()

    @pl.loop(0, tiles)
    def _(t):
        packed[pl.ds(t * CAP, CAP), :] = jnp.zeros((CAP, FEAT), f32)

    @pl.loop(0, rows // 32)
    def _(t):
        part = pl.ds(t * 32, 32)
        xf[part, :] = vis_ref[part, :].astype(f32)

    copy.wait()
    step = 32

    for b in range(blocks):

        @pl.loop(0, BLK // step)
        def _(t):
            for j in range(step):
                at = t * step + j
                packed[pl.ds(slot_s[b, at], 1), :] = xf[pl.ds(b * BLK + at, 1), :]

    @pl.loop(0, tiles)
    def _(t):
        rows_t = packed[pl.ds(t * CAP, CAP), :]
        meta_t = jnp.broadcast_to(meta[pl.ds(t, 1), :], (SENT - CAP, FEAT))
        out_ref[t] = jnp.concatenate([rows_t, meta_t], 0).astype(bf16)


def pack(visibility, destination, cell_u, cell_v, tap_u, tap_v, tiles):
    rows = visibility.shape[0]
    row = lambda x: x.reshape(1, rows)
    return pl.pallas_call(
        pack_kernel,
        out_shape=jax.ShapeDtypeStruct((tiles, SENT, FEAT), bf16),
        scratch_shapes=[
            pltpu.VMEM((rows // BLK, BLK), i32),
            pltpu.SMEM((rows // BLK, BLK), i32),
            pltpu.VMEM((rows, FEAT), f32),
            pltpu.VMEM((tiles * CAP, FEAT), f32),
            pltpu.VMEM((tiles, FEAT), f32),
            pltpu.SemaphoreType.DMA(()),
        ],
        compiler_params=pltpu.CompilerParams(vmem_limit_bytes=VMEM_LIMIT),
        name="pack_rows",
    )(row(destination), row(cell_u), row(cell_v), row(tap_u), row(tap_v), visibility)


def grid_kernel(
    recv_ref, table_ref, out_hbm, ve_ref, ue_ref,
    xf, xm, xs, ms, meta, meta_t, pos_v, pos_s, span_v, span_s, grid, stage, sems, out_sems,
):
    sources = recv_ref.shape[0]
    slots = sources * CAP
    blocks = slots // BLK
    lanes = BLK // sources

    @pl.loop(0, sources)
    def _(s):
        x = recv_ref[s].astype(f32)
        xf[pl.ds(s * CAP, CAP), :] = x[:CAP]
        meta[pl.ds(s, 1), :] = x[CAP:CAP + 1]

    placed = meta[...]
    meta_t[...] = placed.T
    keys = 64

    def key_row(b):
        out = []
        for k in range(b * lanes, (b + 1) * lanes):
            cu1 = meta_t[pl.ds(k, 1), :].astype(i32)
            cv1 = meta_t[pl.ds(CAP + k, 1), :].astype(i32)
            out.append(jnp.where(cu1 > 0, (cv1 - 1) >> 1, keys))
        return jnp.concatenate(out, 1)

    key_ids = iota((128, BLK), 0)
    total = jnp.zeros((128, BLK), f32)
    for b in range(blocks):
        total = total + (key_ids == key_row(b)).astype(f32)
    total = jnp.broadcast_to(jnp.sum(total, 1, keepdims=True), (128, 128))
    below = (iota((128, 128), 1) < iota((128, 128), 0)).astype(f32).astype(bf16)
    high = jnp.floor(total * (1.0 / 64.0))
    low = total - 64.0 * high
    start = 64.0 * dot(below, high.astype(bf16)) + dot(below, low.astype(bf16))
    count = start[keys:keys + 1, :]
    lane = iota((128, 128), 1).astype(f32) * BLK
    real = iota((128, 128), 0) < keys
    first = jnp.sum(jnp.where(real & (start + total <= lane), 1.0, 0.0), 0, keepdims=True)
    last = jnp.sum(jnp.where(real & (start < jnp.minimum(lane + BLK, count)), 1.0, 0.0), 0, keepdims=True) - 1.0
    span_v[...] = jnp.concatenate([first, last, count, jnp.zeros((5, 128), f32)], 0).astype(i32)
    span_copy = pltpu.make_async_copy(span_v, span_s, sems.at[0])
    span_copy.start()
    before = earlier(BLK)
    base = start[:, 0:1]
    for b in range(blocks):
        mine = (key_ids == key_row(b)).astype(f32)
        pos = jnp.sum(mine * (dot(mine.astype(bf16), before) + base), 0, keepdims=True)
        pos_v[pl.ds(b, 1), :] = pos.astype(i32)
        base = base + jnp.sum(mine, 1, keepdims=True)
    pos_copy = pltpu.make_async_copy(pos_v, pos_s, sems.at[1])
    pos_copy.start()
    for k in range(CAP):
        xm[pl.ds(k * sources, sources), :] = pltpu.roll(placed, (FEAT - k) % FEAT, 1)

    @pl.loop(0, EV)
    def _(t):
        grid[pl.ds(t * EU, EU), :] = jnp.zeros((EU, FEAT), f32)

    pos_copy.wait()
    span_copy.wait()

    @pl.loop(0, sources)
    def _(s):
        for k in range(CAP):
            p = pos_s[k // lanes, (k % lanes) * sources + s]
            xs[pl.ds(p, 1), :] = xf[pl.ds(s * CAP + k, 1), :]
            ms[pl.ds(p, 1), :] = xm[pl.ds(k * sources + s, 1), :]

    table_tr = table_ref[...]
    pick = (iota((8, FEAT), 1) == CAP * iota((8, FEAT), 0)).astype(f32).astype(bf16)
    phase_ids = iota((128, BLK), 0)
    u_ids = iota((EU, BLK), 0)
    t_ids = iota((8, BLK), 0)

    @pl.loop(0, (span_s[2, 0] + BLK - 1) // BLK)
    def _(c):
        part = pl.ds(c * BLK, BLK)
        fields = lax.dot_general(pick, ms[part, :].astype(bf16), NT, preferred_element_type=f32).astype(i32) - 1
        cu, cv, tu, tv = (fields[i:i + 1] for i in range(4))
        ku = dot(table_tr, (phase_ids == tu).astype(f32).astype(bf16))
        kv = dot(table_tr, (phase_ids == tv).astype(f32).astype(bf16))
        off = u_ids - (cu + 4)
        wu = jnp.zeros((EU, BLK), f32)
        for a in range(TAPS):
            wu = jnp.where(off == a, ku[a:a + 1], wu)
        wu = wu.astype(bf16)
        v_first = 2 * span_s[0, c]
        steps = 2 * (span_s[1, c] - span_s[0, c]) + TAPS + 1

        @pl.loop(0, (steps + GROUP - 1) // GROUP)
        def _(g):
            v_at = v_first + g * GROUP
            off_v = (t_ids + v_at) - cv
            wv = jnp.zeros((8, BLK), f32)
            for a in range(TAPS):
                wv = jnp.where(off_v == a, kv[a:a + 1], wv)
            wv = wv.T
            x = xs[part, :]
            for j in range(0, GROUP, 2):
                rhs = jnp.concatenate([x * wv[:, j:j + 1], x * wv[:, j + 1:j + 2]], 1).astype(bf16)
                add = dot(wu, rhs)
                for i in range(2):
                    at = pl.ds((v_at + j + i) * EU, EU)
                    grid[at, :] = grid[at, :] + add[:, i * FEAT:(i + 1) * FEAT]

    ve_ref[0] = grid[pl.ds(0, PAD * EU), :]
    ve_ref[1] = grid[pl.ds((TV + PAD) * EU, PAD * EU), :]

    def turned(u):
        return [grid[pl.ds((PAD + 8 * t) * EU + u, 8, stride=EU), :] for t in range(TV // 8)]

    for u in range(PAD):
        for e, at in enumerate((PAD + u, TU + 8 + u)):
            ue_ref[e, u] = jnp.concatenate(turned(at), 0)

    many = 8

    def out_copy(t, slot):
        return pltpu.make_async_copy(stage.at[slot], out_hbm.at[pl.ds(t * many, many)], out_sems.at[slot])

    @pl.loop(0, TU // many)
    def _(t):
        slot = t % 2

        @pl.when(t >= 2)
        def _():
            out_copy(t - 2, slot).wait()

        for u in range(many):
            stage[slot, u] = jnp.concatenate(turned(8 + t * many + u), 0)
        out_copy(t, slot).start()

    for t in (TU // many - 2, TU // many - 1):
        out_copy(t, t % 2).wait()


def grid_rows(recv, table):
    sources = recv.shape[0]
    slots = sources * CAP
    vmem = pl.BlockSpec(memory_space=pltpu.VMEM)
    return pl.pallas_call(
        grid_kernel,
        in_specs=[vmem, vmem],
        out_specs=(pl.BlockSpec(memory_space=pl.ANY), vmem, vmem),
        out_shape=(
            jax.ShapeDtypeStruct((TU, TV, FEAT), f32),
            jax.ShapeDtypeStruct((2, PAD * EU, FEAT), f32),
            jax.ShapeDtypeStruct((2, PAD, TV, FEAT), f32),
        ),
        scratch_shapes=[
            pltpu.VMEM((slots, FEAT), f32),
            pltpu.VMEM((slots, FEAT), f32),
            pltpu.VMEM((slots, FEAT), f32),
            pltpu.VMEM((slots, FEAT), f32),
            pltpu.VMEM((sources, FEAT), f32),
            pltpu.VMEM((FEAT, sources), f32),
            pltpu.VMEM((slots // BLK, BLK), i32),
            pltpu.SMEM((slots // BLK, BLK), i32),
            pltpu.VMEM((8, 128), i32),
            pltpu.SMEM((8, 128), i32),
            pltpu.VMEM((EV * EU, FEAT), f32),
            pltpu.VMEM((2, 8, TV, FEAT), f32),
            pltpu.SemaphoreType.DMA((2,)),
            pltpu.SemaphoreType.DMA((2,)),
        ],
        compiler_params=pltpu.CompilerParams(vmem_limit_bytes=VMEM_LIMIT),
        name="grid_rows",
    )(recv, table)


def shifted(x, axis, up):
    n = lax.axis_size(axis)
    pairs = [(i, i + 1) if up else (i + 1, i) for i in range(n - 1)]
    return lax.ppermute(x, axis, pairs)


def local(visibility, destination, cell_u, cell_v, tap_u, tap_v, kernel_table):
    axes = ("au", "vert")
    tiles = lax.axis_size("au") * lax.axis_size("vert")
    sent = pack(visibility, destination, cell_u, cell_v, tap_u, tap_v, tiles)
    recv = lax.all_to_all(sent, axes, split_axis=0, concat_axis=0, tiled=True)
    out, ve, ue = grid_rows(recv, kernel_table.T)
    v_low = shifted(ve[1], "vert", True).reshape(PAD, EU, FEAT).transpose(1, 0, 2)
    v_high = shifted(ve[0], "vert", False).reshape(PAD, EU, FEAT).transpose(1, 0, 2)
    for e, at in enumerate((PAD, TU + 8)):
        ue = ue.at[e, :, 0:PAD].add(v_low[at:at + PAD])
        ue = ue.at[e, :, TV - PAD:TV].add(v_high[at:at + PAD])
    u_low = shifted(ue[1], "au", True)
    u_high = shifted(ue[0], "au", False)
    out = out.at[:, 0:PAD].add(v_low[8:8 + TU])
    out = out.at[:, TV - PAD:TV].add(v_high[8:8 + TU])
    out = out.at[0:PAD].add(u_low)
    out = out.at[TU - PAD:TU].add(u_high)
    return out


def solution(mesh):
    rows = P(("au", "vert"))
    return jax.shard_map(
        local,
        mesh=mesh,
        in_specs=(P(("au", "vert"), None), P(("au", "vert"), None), rows, rows, rows, rows, P()),
        out_specs=P("au", "vert", None),
        check_vma=False,
    )
```

time: 340 us -> 152 us (0.45)
  the two profiles are of different devices: /device:TPU:1 before, /device:TPU:25 now
where the time goes in v1:
time: 152 us; the launch traced here: 149 us
  Pallas kernels  57.4 us (38%)
  starting transfers between devices  31.4 us (21%)
  blocking collectives  31 us (20%)
  other arithmetic  16.1 us (11%)
  waiting for transfers between devices  7.91 us (5%)
  local copies, waits for them, and re-layouts  5.57 us (4%)
    pallas_call x1, Pallas kernels, grid_rows(): pl.pallas_call(grid_kernel, in_specs=[vmem, vmem], out_specs=(pl.BlockSpe...  47.9 us
    ppermute x4, starting transfers between devices, shifted(): return lax.ppermute(x, axis, pairs)  31.4 us
    all_to_all x1, blocking collectives, local(): recv = lax.all_to_all(sent, axes, split_axis=0, concat_axis=0, tiled=True)  31 us
    pallas_call x1, Pallas kernels, pack(): pl.pallas_call(pack_kernel, out_shape=jax.ShapeDtypeStruct((tiles, SENT,...  9.43 us
    ppermute x4, waiting for transfers between devices, shifted(): return lax.ppermute(x, axis, pairs)  7.91 us
    another operation x3, other arithmetic  5.15 us
  transfers between devices with their start and end apart: 4, of which 2 were waited for; matrix products, arithmetic and copies ran while one was open for 6% of the time, Pallas kernels for 0%

profile of v1, /device:TPU:25, one launch (start us, length us, event | category | flops | bytes accessed | tf_op | source)
XLA Modules:
  0.0 149.5 jit_solution(6728789513693942474)
XLA Ops:
  0.0 9.4 %pack_rows.1 = bf16[128,40,128]{2,1,0:T(8,128)(2,1)} custom-call(s32[1,2048]{1,0:T(1,128)} %bitcast.54, s32[1,2048]{1,0:T(1,128)} %bitcast.55, s32[1,2048]{1,0:T(1,128)} %bitcast.56, s32[1,2048]{1,0:T(1,128)} %bitcast.57, s32[1,2048]{1,0:T(1,128)} %bitcast.58, bf16[2048,128]{1,0:T(8,128)(2,1)} %vis_ref.1), custom_call_target="tpu_custom_call" | custom-call | tf_op jit(solution)/shard_map/pack_rows/pallas_call | solution.py:97
  9.4 31.0 %all_to_all.5.recv_ref = bf16[128,40,128]{2,1,0:T(8,128)(2,1)} all-to-all(bf16[128,40,128]{2,1,0:T(8,128)(2,1)} %pack_rows.1), channel_id=1, replica_groups=mesh['au'=16,'vert'=8] {'au','vert'}, dimensions={0} | all-to-all | bytes 2621440 | tf_op jit(solution)/shard_map/all_to_all | solution.py:295
  40.4 47.9 %grid_rows.1 = (f32[128,128,128]{2,1,0:T(8,128)}, f32[2,576,128]{2,1,0:T(8,128)}, f32[2,4,128,128]{3,2,1,0:T(8,128)}) custom-call(bf16[128,40,128]{2,1,0:T(8,128)(2,1)} %all_to_all.5.recv_ref, bf16[8,128]{1,0:T(8,128)(2,1)} %bitcast.59), custom_call_target="tpu_custom_call" | custom-call | tf_op jit(solution)/shard_map/grid_rows/pallas_call | solution.py:255
  88.4 1.1 slice_bitcast_fusion
  89.5 4.2 %collective-permute-start = (f32[576,128]{1,0:T(8,128)S(1)}, f32[576,128]{1,0:T(8,128)S(1)}, u32[]{:S(2)}, u32[]{:S(2)}) collective-permute-start(f32[576,128]{1,0:T(8,128)S(1)} %get-tuple-element.108), channel_id=1, source_target_pairs={{0,1},{1,2},{2,3},{3,4},{4,5},{5,6},{6,7},{8,9},{9,10},{10,11},{11... | collective-permute-start | bytes 884744 | tf_op jit(solution)/shard_map/ppermute | solution.py:288
  93.7 1.9 %collective-permute-start.1 = (f32[576,128]{1,0:T(8,128)S(1)}, f32[576,128]{1,0:T(8,128)S(1)}, u32[]{:S(2)}, u32[]{:S(2)}) collective-permute-start(f32[576,128]{1,0:T(8,128)S(1)} %get-tuple-element.107), channel_id=1, source_target_pairs={{1,0},{2,1},{3,2},{4,3},{5,4},{6,5},{7,6},{9,8},{10,9},{11,10},{12... | collective-permute-start | bytes 884744 | tf_op jit(solution)/shard_map/ppermute | solution.py:288
  95.6 0.6 fusion.10
  96.2 2.6 %and_reduce_fusion = pred[]{:T(512)} fusion(s32[4]{0:T(128)} %constant.221.clone.1, s32[1]{0:T(128)} %constant.220.clone.1, s32[1]{0:T(128)} %get-tuple-element.111, s32[1]{0:T(128)} %get-tuple-element.112), kind=kLoop, calls=%fused_computation.25 | loop fusion | flops 27 | bytes 29 | tf_op jit(solution)/shard_map/reduce.11
  98.9 0.0 collective-permute-done
  98.9 0.1 copy.13
  99.0 3.3 %collective-permute-done.1 = f32[576,128]{1,0:T(8,128)S(1)} collective-permute-done((f32[576,128]{1,0:T(8,128)S(1)}, f32[576,128]{1,0:T(8,128)S(1)}, u32[]{:S(2)}, u32[]{:S(2)}) %collective-permute-start.1) | collective-permute-done | bytes 294944 | tf_op jit(solution)/shard_map/ppermute | solution.py:288
  102.3 0.1 copy.12
  102.4 1.3 fusion.9
  103.7 2.5 %add_select_fusion = f32[1,4,4,128]{3,2,1,0:T(4,128)S(1)} fusion(f32[144,4,128]{2,1,0:T(4,128)S(1)} %bitcast.46, f32[2,4,128,128]{3,2,1,0:T(8,128)} %fusion.9, s32[]{:T(128)} %bitcast.13, s32[]{:T(128)} %bitcast.14, pred[]{:T(512)} %and_reduce_fusion), kind=kLoop, calls=%fused_computation.14 | loop fusion | flops 4096 | bytes 24585 | tf_op jit(solution)/shard_map/select.11
  106.3 2.6 %scatter-add.31 = f32[2,4,128,128]{3,2,1,0:T(8,128)} dynamic-update-slice(f32[2,4,128,128]{3,2,1,0:T(8,128)} %fusion.9, f32[1,4,4,128]{3,2,1,0:T(4,128)S(1)} %add_select_fusion, s32[]{:T(128)} %bitcast.13, s32[]{:T(128)} %constant.218.clone.1, s32[]{:T(128)} %bitcast.14, s32[]{:T(128)} %constant.218.clone.1) | dynamic-update-slice | bytes 16388 | tf_op jit(solution)/shard_map/scatter-add | solution.py:301
  108.9 1.3 fusion.7
  110.2 1.3 fusion.5
  111.5 1.1 slice_bitcast_fusion.2
  112.6 21.3 %collective-permute-start.2 = (f32[4,128,128]{2,1,0:T(8,128)S(1)}, f32[4,128,128]{2,1,0:T(8,128)S(1)}, u32[]{:S(2)}, u32[]{:S(2)}) collective-permute-start(f32[4,128,128]{2,1,0:T(8,128)S(1)} %get-tuple-element.110), channel_id=1, source_target_pairs={{0,8},{8,16},{16,24},{24,32},{32,40},{40,48},{48,56},{56,64},{64,7... | collective-permute-start | bytes 786440 | tf_op jit(solution)/shard_map/ppermute | solution.py:288
  133.8 1.8 %fusion.3 = f32[128,128,128]{2,1,0:T(8,128)} fusion(f32[128,128,128]{2,1,0:T(8,128)} %get-tuple-element.104, f32[144,4,128]{2,1,0:T(4,128)S(1)} %bitcast.51), kind=kLoop, calls=%fused_computation.13 | loop fusion | flops 65536 | bytes 786432 | tf_op jit(solution)/shard_map/scatter-add | solution.py:304
  135.6 4.0 %collective-permute-start.3 = (f32[4,128,128]{2,1,0:T(8,128)S(1)}, f32[4,128,128]{2,1,0:T(8,128)S(1)}, u32[]{:S(2)}, u32[]{:S(2)}) collective-permute-start(f32[4,128,128]{2,1,0:T(8,128)S(1)} %get-tuple-element.109), channel_id=1, source_target_pairs={{8,0},{16,8},{24,16},{32,24},{40,32},{48,40},{56,48},{64,56},{72,6... | collective-permute-start | bytes 786440 | tf_op jit(solution)/shard_map/ppermute | solution.py:288
  139.7 1.8 %fusion.2 = f32[128,128,128]{2,1,0:T(8,128)} fusion(f32[128,128,128]{2,1,0:T(8,128)} %fusion.3, f32[144,4,128]{2,1,0:T(4,128)S(1)} %bitcast.48), kind=kLoop, calls=%fused_computation.11 | loop fusion | flops 65536 | bytes 786432 | tf_op jit(solution)/shard_map/scatter-add | solution.py:305
  141.5 0.0 collective-permute-done.2
  141.5 1.7 %fusion.1 = f32[128,128,128]{2,1,0:T(8,128)} fusion(f32[128,128,128]{2,1,0:T(8,128)} %fusion.2, f32[4,128,128]{2,1,0:T(8,128)S(1)} %collective-permute-done.2), kind=kLoop, calls=%fused_computation.9 | loop fusion | flops 65536 | bytes 786432 | tf_op jit(solution)/shard_map/scatter-add | solution.py:306
  143.2 4.6 %collective-permute-done.3 = f32[4,128,128]{2,1,0:T(8,128)S(1)} collective-permute-done((f32[4,128,128]{2,1,0:T(8,128)S(1)}, f32[4,128,128]{2,1,0:T(8,128)S(1)}, u32[]{:S(2)}, u32[]{:S(2)}) %collective-permute-start.3) | collective-permute-done | bytes 262176 | tf_op jit(solution)/shard_map/ppermute | solution.py:288
  147.8 1.7 %fusion = f32[128,128,128]{2,1,0:T(8,128)} fusion(f32[128,128,128]{2,1,0:T(8,128)} %fusion.1, f32[4,128,128]{2,1,0:T(8,128)S(1)} %collective-permute-done.3), kind=kLoop, calls=%fused_computation.6 | loop fusion | flops 65536 | bytes 786432 | tf_op jit(solution)/shard_map/scatter-add | solution.py:307
  (1 shorter events, 0.0 us)
Async XLA Ops:
  89.5 9.4 %collective-permute-start = (f32[576,128]{1,0:T(8,128)S(1)}, f32[576,128]{1,0:T(8,128)S(1)}, u32[]{:S(2)}, u32[]{:S(2)}) collective-permute-start(f32[576,128]{1,0:T(8,128)S(1)} %get-tuple-element.108), channel_id=1, source_target_pairs={{0,1},{1,2},{2,3},{3,4},{4,5},{5,6},{6,7},{8,9},{9,10},{10,11},{11... | collective-permute-start | bytes 884744 | tf_op jit(solution)/shard_map/ppermute | solution.py:288
  93.7 8.6 %collective-permute-start.1 = (f32[576,128]{1,0:T(8,128)S(1)}, f32[576,128]{1,0:T(8,128)S(1)}, u32[]{:S(2)}, u32[]{:S(2)}) collective-permute-start(f32[576,128]{1,0:T(8,128)S(1)} %get-tuple-element.107), channel_id=1, source_target_pairs={{1,0},{2,1},{3,2},{4,3},{5,4},{6,5},{7,6},{9,8},{10,9},{11,10},{12... | collective-permute-start | bytes 884744 | tf_op jit(solution)/shard_map/ppermute | solution.py:288
  112.6 28.9 %collective-permute-start.2 = (f32[4,128,128]{2,1,0:T(8,128)S(1)}, f32[4,128,128]{2,1,0:T(8,128)S(1)}, u32[]{:S(2)}, u32[]{:S(2)}) collective-permute-start(f32[4,128,128]{2,1,0:T(8,128)S(1)} %get-tuple-element.110), channel_id=1, source_target_pairs={{0,8},{8,16},{16,24},{24,32},{32,40},{40,48},{48,56},{56,64},{64,7... | collective-permute-start | bytes 786440 | tf_op jit(solution)/shard_map/ppermute | solution.py:288
  135.6 12.1 %collective-permute-start.3 = (f32[4,128,128]{2,1,0:T(8,128)S(1)}, f32[4,128,128]{2,1,0:T(8,128)S(1)}, u32[]{:S(2)}, u32[]{:S(2)}) collective-permute-start(f32[4,128,128]{2,1,0:T(8,128)S(1)} %get-tuple-element.109), channel_id=1, source_target_pairs={{8,0},{16,8},{24,16},{32,24},{40,32},{48,40},{56,48},{64,56},{72,6... | collective-permute-start | bytes 786440 | tf_op jit(solution)/shard_map/ppermute | solution.py:288

commit v2 on v1

--- a/solution.py
+++ b/solution.py
@@ -13,10 +13,10 @@
 SENT = CAP + 8
 BLK = 256
 EU = 144
-EV = 144
+EV = 160
 PAD = 4
-GROUP = 4
-VMEM_LIMIT = 56 * 1024 * 1024
+GROUP = 20
+MIB = 1024 * 1024
 NT = (((1,), (1,)), ((), ()))
 
 f32 = jnp.float32
@@ -105,15 +105,16 @@
             pltpu.VMEM((tiles, FEAT), f32),
             pltpu.SemaphoreType.DMA(()),
         ],
-        compiler_params=pltpu.CompilerParams(vmem_limit_bytes=VMEM_LIMIT),
+        compiler_params=pltpu.CompilerParams(vmem_limit_bytes=16 * MIB),
         name="pack_rows",
     )(row(destination), row(cell_u), row(cell_v), row(tap_u), row(tap_v), visibility)
 
 
 def grid_kernel(
-    recv_ref, table_ref, out_hbm, ve_ref, ue_ref,
-    xf, xm, xs, ms, meta, meta_t, pos_v, pos_s, span_v, span_s, grid, stage, sems, out_sems,
+    recv_ref, table_ref, out_hbm, ve_low, ve_high, ue_ref,
+    xf, xm, xs, ms, meta, meta_t, pos_v, pos_s, span_v, span_s, wu, taps_v, grid3, sems, out_sems,
 ):
+    grid = grid3.reshape(EV * EU, FEAT)
     sources = recv_ref.shape[0]
     slots = sources * CAP
     blocks = slots // BLK
@@ -184,9 +185,10 @@
     pick = (iota((8, FEAT), 1) == CAP * iota((8, FEAT), 0)).astype(f32).astype(bf16)
     phase_ids = iota((128, BLK), 0)
     u_ids = iota((EU, BLK), 0)
-    t_ids = iota((8, BLK), 0)
-
-    @pl.loop(0, (span_s[2, 0] + BLK - 1) // BLK)
+    t_ids = iota((GROUP + 4, BLK), 0)
+    chunks = (span_s[2, 0] + BLK - 1) // BLK
+
+    @pl.loop(0, chunks)
     def _(c):
         part = pl.ds(c * BLK, BLK)
         fields = lax.dot_general(pick, ms[part, :].astype(bf16), NT, preferred_element_type=f32).astype(i32) - 1
@@ -194,58 +196,58 @@
         ku = dot(table_tr, (phase_ids == tu).astype(f32).astype(bf16))
         kv = dot(table_tr, (phase_ids == tv).astype(f32).astype(bf16))
         off = u_ids - (cu + 4)
-        wu = jnp.zeros((EU, BLK), f32)
+        weights = jnp.zeros((EU, BLK), f32)
         for a in range(TAPS):
-            wu = jnp.where(off == a, ku[a:a + 1], wu)
-        wu = wu.astype(bf16)
+            weights = jnp.where(off == a, ku[a:a + 1], weights)
+        wu[c] = weights.astype(bf16)
+        taps_v[c, 0:8] = kv
+        taps_v[c, 8:16] = jnp.broadcast_to(cv, (8, BLK)).astype(f32)
+
+    @pl.loop(0, chunks)
+    def _(c):
         v_first = 2 * span_s[0, c]
         steps = 2 * (span_s[1, c] - span_s[0, c]) + TAPS + 1
 
         @pl.loop(0, (steps + GROUP - 1) // GROUP)
         def _(g):
+            x = xs[pl.ds(c * BLK, BLK), :].astype(bf16)
             v_at = v_first + g * GROUP
-            off_v = (t_ids + v_at) - cv
-            wv = jnp.zeros((8, BLK), f32)
+            off_v = (t_ids + v_at) - taps_v[c, 8:9].astype(i32)
+            wv = jnp.zeros((GROUP + 4, BLK), f32)
             for a in range(TAPS):
-                wv = jnp.where(off_v == a, kv[a:a + 1], wv)
-            wv = wv.T
-            x = xs[part, :]
+                wv = jnp.where(off_v == a, taps_v[c, a:a + 1], wv)
+            wv = wv.T.astype(bf16)
             for j in range(0, GROUP, 2):
-                rhs = jnp.concatenate([x * wv[:, j:j + 1], x * wv[:, j + 1:j + 2]], 1).astype(bf16)
-                add = dot(wu, rhs)
+                rhs = jnp.concatenate([x * wv[:, j:j + 1], x * wv[:, j + 1:j + 2]], 1)
+                add = dot(wu[c], rhs)
                 for i in range(2):
                     at = pl.ds((v_at + j + i) * EU, EU)
                     grid[at, :] = grid[at, :] + add[:, i * FEAT:(i + 1) * FEAT]
 
-    ve_ref[0] = grid[pl.ds(0, PAD * EU), :]
-    ve_ref[1] = grid[pl.ds((TV + PAD) * EU, PAD * EU), :]
-
-    def turned(u):
-        return [grid[pl.ds((PAD + 8 * t) * EU + u, 8, stride=EU), :] for t in range(TV // 8)]
-
-    for u in range(PAD):
-        for e, at in enumerate((PAD + u, TU + 8 + u)):
-            ue_ref[e, u] = jnp.concatenate(turned(at), 0)
-
-    many = 8
-
-    def out_copy(t, slot):
-        return pltpu.make_async_copy(stage.at[slot], out_hbm.at[pl.ds(t * many, many)], out_sems.at[slot])
-
-    @pl.loop(0, TU // many)
-    def _(t):
-        slot = t % 2
-
-        @pl.when(t >= 2)
-        def _():
-            out_copy(t - 2, slot).wait()
-
-        for u in range(many):
-            stage[slot, u] = jnp.concatenate(turned(8 + t * many + u), 0)
-        out_copy(t, slot).start()
-
-    for t in (TU // many - 2, TU // many - 1):
-        out_copy(t, t % 2).wait()
+    def out_copy(u):
+        return pltpu.make_async_copy(grid3.at[pl.ds(PAD, TV), 8 + u], out_hbm.at[u], out_sems.at[0])
+
+    @pl.loop(0, TU)
+    def _(u):
+        out_copy(u).start()
+
+    ve_low[...] = grid[pl.ds(0, PAD * EU), :].astype(bf16)
+    ve_high[...] = grid[pl.ds((TV + PAD) * EU, PAD * EU), :].astype(bf16)
+
+    def edge_copy(e, u):
+        at = (PAD, TU + 8)[e] + u
+        return pltpu.make_async_copy(grid3.at[pl.ds(PAD, TV), at], ue_ref.at[e, u], out_sems.at[1])
+
+    for e in range(2):
+        for u in range(PAD):
+            edge_copy(e, u).start()
+    for e in range(2):
+        for u in range(PAD):
+            edge_copy(e, u).wait()
+
+    @pl.loop(0, TU)
+    def _(u):
+        out_copy(u).wait()
 
 
 def grid_rows(recv, table):
@@ -255,10 +257,11 @@
     return pl.pallas_call(
         grid_kernel,
         in_specs=[vmem, vmem],
-        out_specs=(pl.BlockSpec(memory_space=pl.ANY), vmem, vmem),
+        out_specs=(pl.BlockSpec(memory_space=pl.ANY), vmem, vmem, vmem),
         out_shape=(
             jax.ShapeDtypeStruct((TU, TV, FEAT), f32),
-            jax.ShapeDtypeStruct((2, PAD * EU, FEAT), f32),
+            jax.ShapeDtypeStruct((PAD * EU, FEAT), bf16),
+            jax.ShapeDtypeStruct((PAD * EU, FEAT), bf16),
             jax.ShapeDtypeStruct((2, PAD, TV, FEAT), f32),
         ),
         scratch_shapes=[
@@ -272,14 +275,124 @@
             pltpu.SMEM((slots // BLK, BLK), i32),
             pltpu.VMEM((8, 128), i32),
             pltpu.SMEM((8, 128), i32),
-            pltpu.VMEM((EV * EU, FEAT), f32),
-            pltpu.VMEM((2, 8, TV, FEAT), f32),
+            pltpu.VMEM((slots // BLK, EU, BLK), bf16),
+            pltpu.VMEM((slots // BLK, 16, BLK), f32),
+            pltpu.VMEM((EV, EU, FEAT), f32),
             pltpu.SemaphoreType.DMA((2,)),
             pltpu.SemaphoreType.DMA((2,)),
         ],
-        compiler_params=pltpu.CompilerParams(vmem_limit_bytes=VMEM_LIMIT),
+        compiler_params=pltpu.CompilerParams(vmem_limit_bytes=36 * MIB),
         name="grid_rows",
     )(recv, table)
+
+
+def corner_kernel(low_ref, high_ref, ue_ref, send_low, send_high, low, high, edges):
+    edges[...] = ue_ref[...]
+    low[...] = low_ref[...].astype(f32)
+    high[...] = high_ref[...].astype(f32)
+    for e, (at, send) in enumerate(((PAD, send_low), (TU + 8, send_high))):
+        for u in range(PAD):
+            there = pl.ds(at + u, PAD, stride=EU)
+            edges[e, u, 0:PAD, :] += low[there, :]
+            edges[e, u, TV - PAD:TV, :] += high[there, :]
+        send[...] = edges[e].astype(bf16)
+
+
+def add_corners(low, high, ue):
+    edge = jax.ShapeDtypeStruct(ue.shape[1:], bf16)
+    return pl.pallas_call(
+        corner_kernel,
+        out_shape=(edge, edge),
+        scratch_shapes=[
+            pltpu.VMEM(low.shape, f32),
+            pltpu.VMEM(high.shape, f32),
+            pltpu.VMEM(ue.shape, f32),
+        ],
+        compiler_params=pltpu.CompilerParams(vmem_limit_bytes=8 * MIB),
+        name="add_corners",
+    )(low, high, ue)
+
+
+def v_edge_kernel(out_in, low_ref, high_ref, out_hbm, own_ref, low, high, edges, sems):
+    def copy(e, back):
+        there = out_hbm.at[:, pl.ds(e * (TV - 8), 8)]
+        ends = (edges.at[e], there) if back else (there, edges.at[e])
+        return pltpu.make_async_copy(*ends, sems.at[e])
+
+    copy(0, False).start()
+    copy(1, False).start()
+    low[...] = low_ref[...].astype(f32)
+    high[...] = high_ref[...].astype(f32)
+    for e, (halo, at) in enumerate(((low, 0), (high, 8 - PAD))):
+        copy(e, False).wait()
+
+        @pl.loop(0, TU // 8)
+        def _(t):
+            for j in range(8):
+                u = t * 8 + j
+                edges[e, u, at:at + PAD, :] += halo[pl.ds(8 + u, PAD, stride=EU), :]
+
+        copy(e, True).start()
+    copy(0, True).wait()
+    copy(1, True).wait()
+    own = [
+        pltpu.make_async_copy(out_hbm.at[pl.ds(e * (TU - PAD), PAD)], own_ref.at[e], sems.at[e])
+        for e in range(2)
+    ]
+    own[0].start()
+    own[1].start()
+    own[0].wait()
+    own[1].wait()
+
+
+def add_v_edges(out, low, high):
+    vmem = pl.BlockSpec(memory_space=pltpu.VMEM)
+    hbm = pl.BlockSpec(memory_space=pl.ANY)
+    return pl.pallas_call(
+        v_edge_kernel,
+        in_specs=[hbm, vmem, vmem],
+        out_specs=(hbm, vmem),
+        out_shape=(
+            jax.ShapeDtypeStruct(out.shape, f32),
+            jax.ShapeDtypeStruct((2, PAD, TV, FEAT), f32),
+        ),
+        scratch_shapes=[
+            pltpu.VMEM(low.shape, f32),
+            pltpu.VMEM(high.shape, f32),
+            pltpu.VMEM((2, TU, 8, FEAT), f32),
+            pltpu.SemaphoreType.DMA((2,)),
+        ],
+        input_output_aliases={0: 0},
+        compiler_params=pltpu.CompilerParams(vmem_limit_bytes=8 * MIB),
+        name="add_v_edges",
+    )(out, low, high)
+
+
+def u_edge_kernel(out_in, low_ref, high_ref, own_ref, out_hbm, edges, sems):
+    def copy(e):
+        return pltpu.make_async_copy(edges.at[e], out_hbm.at[pl.ds(e * (TU - PAD), PAD)], sems.at[e])
+
+    edges[0] = own_ref[0] + low_ref[...].astype(f32)
+    copy(0).start()
+    edges[1] = own_ref[1] + high_ref[...].astype(f32)
+    copy(1).start()
+    copy(0).wait()
+    copy(1).wait()
+
+
+def add_u_edges(out, low, high, own):
+    vmem = pl.BlockSpec(memory_space=pltpu.VMEM)
+    hbm = pl.BlockSpec(memory_space=pl.ANY)
+    return pl.pallas_call(
+        u_edge_kernel,
+        in_specs=[hbm, vmem, vmem, vmem],
+        out_specs=hbm,
+        out_shape=jax.ShapeDtypeStruct(out.shape, f32),
+        scratch_shapes=[pltpu.VMEM(own.shape, f32), pltpu.SemaphoreType.DMA((2,))],
+        input_output_aliases={0: 0},
+        compiler_params=pltpu.CompilerParams(vmem_limit_bytes=8 * MIB),
+        name="add_u_edges",
+    )(out, low, high, own)
 
 
 def shifted(x, axis, up):
@@ -293,19 +406,14 @@
     tiles = lax.axis_size("au") * lax.axis_size("vert")
     sent = pack(visibility, destination, cell_u, cell_v, tap_u, tap_v, tiles)
     recv = lax.all_to_all(sent, axes, split_axis=0, concat_axis=0, tiled=True)
-    out, ve, ue = grid_rows(recv, kernel_table.T)
-    v_low = shifted(ve[1], "vert", True).reshape(PAD, EU, FEAT).transpose(1, 0, 2)
-    v_high = shifted(ve[0], "vert", False).reshape(PAD, EU, FEAT).transpose(1, 0, 2)
-    for e, at in enumerate((PAD, TU + 8)):
-        ue = ue.at[e, :, 0:PAD].add(v_low[at:at + PAD])
-        ue = ue.at[e, :, TV - PAD:TV].add(v_high[at:at + PAD])
-    u_low = shifted(ue[1], "au", True)
-    u_high = shifted(ue[0], "au", False)
-    out = out.at[:, 0:PAD].add(v_low[8:8 + TU])
-    out = out.at[:, TV - PAD:TV].add(v_high[8:8 + TU])
-    out = out.at[0:PAD].add(u_low)
-    out = out.at[TU - PAD:TU].add(u_high)
-    return out
+    out, ve_low, ve_high, ue = grid_rows(recv, kernel_table.T)
+    v_low = shifted(ve_high, "vert", True)
+    v_high = shifted(ve_low, "vert", False)
+    send_low, send_high = add_corners(v_low, v_high, ue)
+    u_low = shifted(send_high, "au", True)
+    u_high = shifted(send_low, "au", False)
+    out, own = add_v_edges(out, v_low, v_high)
+    return add_u_edges(out, u_low, u_high, own)
 
 
 def solution(mesh):

time: 152 us -> 97.6 us (0.64)
  the two profiles are of different devices: /device:TPU:25 before, /device:TPU:1 now
where the time goes in v2:
time: 97.6 us; the launch traced here: 97 us
  Pallas kernels  40 us (41%)
  blocking collectives  33.4 us (34%)
  starting transfers between devices  12.6 us (13%)
  waiting for transfers between devices  5.69 us (6%)
  local copies, waits for them, and re-layouts  5.2 us (5%)
    all_to_all x1, blocking collectives, local(): recv = lax.all_to_all(sent, axes, split_axis=0, concat_axis=0, tiled=True)  33.4 us
    pallas_call x1, Pallas kernels, grid_rows(): pl.pallas_call(grid_kernel, in_specs=[vmem, vmem], out_specs=(pl.BlockSpe...  28.7 us
    ppermute x4, starting transfers between devices, shifted(): return lax.ppermute(x, axis, pairs)  12.6 us
    pallas_call x1, Pallas kernels, pack(): pl.pallas_call(pack_kernel, out_shape=jax.ShapeDtypeStruct((tiles, SENT,...  7.19 us
    ppermute x4, waiting for transfers between devices, shifted(): return lax.ppermute(x, axis, pairs)  5.69 us
    unnamed x14, local copies, waits for them, and re-layouts  5.2 us
    pallas_call x1, Pallas kernels, add_v_edges(): pl.pallas_call(v_edge_kernel, in_specs=[hbm, vmem, vmem], out_specs=(hbm,...  3.24 us
  transfers between devices with their start and end apart: 4, of which 3 were waited for; matrix products, arithmetic and copies ran while one was open for 0% of the time, Pallas kernels for 3%

profile of v2, /device:TPU:1, one launch (start us, length us, event | category | flops | bytes accessed | tf_op | source)
XLA Modules:
  0.0 97.0 jit_solution(11942902485865866294)
XLA Ops:
  0.0 0.0 copy-start
  0.0 1.0 %copy-done = bf16[2048,128]{1,0:T(8,128)(2,1)S(1)} copy-done((bf16[2048,128]{1,0:T(8,128)(2,1)S(1)}, bf16[2048,128]{1,0:T(8,128)(2,1)}, u32[]{:S(2)}) %copy-start) | copy-done | bytes 524312
  1.0 0.0 copy-start.1
  1.0 0.7 copy-done.1
  1.7 0.0 copy-start.2
  1.7 0.7 copy-done.2
  2.4 0.0 copy-start.3
  2.4 0.7 copy-done.3
  3.1 0.0 copy-start.4
  3.1 0.7 copy-done.4
  3.8 0.0 copy-start.5
  3.8 0.7 copy-done.5
  4.5 7.2 %pack_rows.1 = bf16[128,40,128]{2,1,0:T(8,128)(2,1)S(1)} custom-call(s32[1,2048]{1,0:T(1,128)S(1)} %bitcast.6, s32[1,2048]{1,0:T(1,128)S(1)} %bitcast.7, s32[1,2048]{1,0:T(1,128)S(1)} %bitcast.8, s32[1,2048]{1,0:T(1,128)S(1)} %bitcast.9, s32[1,2048]{1,0:T(1,128)S(1)} %bitcast.10, bf16[2048,128]{1,0:T(8,128)(2,1)S(1)} %copy-done), custom_call_target="tpu_custom_call" | custom-call | tf_op jit(solution)/shard_map/pack_rows/pallas_call | solution.py:97
  11.7 33.4 %all_to_all.5.recv_ref = bf16[128,40,128]{2,1,0:T(8,128)(2,1)S(1)} all-to-all(bf16[128,40,128]{2,1,0:T(8,128)(2,1)S(1)} %pack_rows.1), channel_id=1, replica_groups=mesh['au'=16,'vert'=8] {'au','vert'}, dimensions={0} | all-to-all | bytes 2621440 | tf_op jit(solution)/shard_map/all_to_all | solution.py:408
  45.1 0.0 copy-start.6
  45.1 0.7 copy-done.6
  45.8 28.7 %grid_rows.1 = (f32[128,128,128]{2,1,0:T(8,128)}, bf16[576,128]{1,0:T(8,128)(2,1)S(1)}, bf16[576,128]{1,0:T(8,128)(2,1)S(1)}, f32[2,4,128,128]{3,2,1,0:T(8,128)S(1)}) custom-call(bf16[128,40,128]{2,1,0:T(8,128)(2,1)S(1)} %all_to_all.5.recv_ref, bf16[8,128]{1,0:T(8,128)(2,1)S(1)} %bitcast.11), custom_call_target="tpu_custom_call" | custom-call | tf_op jit(solution)/shard_map/grid_rows/pallas_call | solution.py:257
  74.5 8.0 %collective-permute-start = (bf16[576,128]{1,0:T(8,128)(2,1)S(1)}, bf16[576,128]{1,0:T(8,128)(2,1)S(1)}, u32[]{:S(2)}, u32[]{:S(2)}) collective-permute-start(bf16[576,128]{1,0:T(8,128)(2,1)S(1)} %get-tuple-element.14), channel_id=1, source_target_pairs={{0,1},{1,2},{2,3},{3,4},{4,5},{5,6},{6,7},{8,9},{9,10},{10,11},{11... | collective-permute-start | bytes 442376 | tf_op jit(solution)/shard_map/ppermute | solution.py:401
  82.6 1.9 %collective-permute-start.1 = (bf16[576,128]{1,0:T(8,128)(2,1)S(1)}, bf16[576,128]{1,0:T(8,128)(2,1)S(1)}, u32[]{:S(2)}, u32[]{:S(2)}) collective-permute-start(bf16[576,128]{1,0:T(8,128)(2,1)S(1)} %get-tuple-element.15), channel_id=1, source_target_pairs={{1,0},{2,1},{3,2},{4,3},{5,4},{6,5},{7,6},{9,8},{10,9},{11,10},{12... | collective-permute-start | bytes 442376 | tf_op jit(solution)/shard_map/ppermute | solution.py:401
  84.5 0.2 collective-permute-done.low_ref
  84.6 4.4 %collective-permute-done.1.high_ref = bf16[576,128]{1,0:T(8,128)(2,1)S(1)} collective-permute-done((bf16[576,128]{1,0:T(8,128)(2,1)S(1)}, bf16[576,128]{1,0:T(8,128)(2,1)S(1)}, u32[]{:S(2)}, u32[]{:S(2)}) %collective-permute-start.1) | collective-permute-done | bytes 147488 | tf_op jit(solution)/shard_map/ppermute | solution.py:401
  89.0 0.1 add_corners.1
  89.1 1.3 %collective-permute-start.2 = (bf16[4,128,128]{2,1,0:T(8,128)(2,1)S(1)}, bf16[4,128,128]{2,1,0:T(8,128)(2,1)S(1)}, u32[]{:S(2)}, u32[]{:S(2)}) collective-permute-start(bf16[4,128,128]{2,1,0:T(8,128)(2,1)S(1)} %get-tuple-element.18), channel_id=1, source_target_pairs={{0,8},{8,16},{16,24},{24,32},{32,40},{40,48},{48,56},{56,64},{64,7... | collective-permute-start | bytes 393224 | tf_op jit(solution)/shard_map/ppermute | solution.py:401
  90.4 1.3 %collective-permute-start.3 = (bf16[4,128,128]{2,1,0:T(8,128)(2,1)S(1)}, bf16[4,128,128]{2,1,0:T(8,128)(2,1)S(1)}, u32[]{:S(2)}, u32[]{:S(2)}) collective-permute-start(bf16[4,128,128]{2,1,0:T(8,128)(2,1)S(1)} %get-tuple-element.19), channel_id=1, source_target_pairs={{8,0},{16,8},{24,16},{32,24},{40,32},{48,40},{56,48},{64,56},{72,6... | collective-permute-start | bytes 393224 | tf_op jit(solution)/shard_map/ppermute | solution.py:401
  91.7 3.2 %add_v_edges.1 = (f32[128,128,128]{2,1,0:T(8,128)}, f32[2,4,128,128]{3,2,1,0:T(8,128)S(1)}) custom-call(f32[128,128,128]{2,1,0:T(8,128)} %get-tuple-element.13.out_in, bf16[576,128]{1,0:T(8,128)(2,1)S(1)} %collective-permute-done.low_ref, bf16[576,128]{1,0:T(8,128)(2,1)S(1)} %collective-permute-done.1.high_ref), custom_call_target="tpu_custom_call", output_to_operand_aliasing={{0}: (0, {})} | custom-call | tf_op jit(solution)/shard_map/add_v_edges/pallas_call | solution.py:351
  95.0 0.0 collective-permute-done.2.low_ref
  95.0 1.2 %collective-permute-done.3.high_ref = bf16[4,128,128]{2,1,0:T(8,128)(2,1)S(1)} collective-permute-done((bf16[4,128,128]{2,1,0:T(8,128)(2,1)S(1)}, bf16[4,128,128]{2,1,0:T(8,128)(2,1)S(1)}, u32[]{:S(2)}, u32[]{:S(2)}) %collective-permute-start.3) | collective-permute-done | bytes 131104 | tf_op jit(solution)/shard_map/ppermute | solution.py:401
  96.1 0.8 add_u_edges.1
Async XLA Ops:
  0.0 1.0 %copy-start = (bf16[2048,128]{1,0:T(8,128)(2,1)S(1)}, bf16[2048,128]{1,0:T(8,128)(2,1)}, u32[]{:S(2)}) copy-start(bf16[2048,128]{1,0:T(8,128)(2,1)} %vis_ref.1) | copy-start | bytes 1572868
  1.0 0.7 copy-start.1
  1.7 0.7 copy-start.2
  2.4 0.7 copy-start.3
  3.1 0.7 copy-start.4
  3.8 0.7 copy-start.5
  45.1 0.7 copy-start.6
  74.5 10.1 %collective-permute-start = (bf16[576,128]{1,0:T(8,128)(2,1)S(1)}, bf16[576,128]{1,0:T(8,128)(2,1)S(1)}, u32[]{:S(2)}, u32[]{:S(2)}) collective-permute-start(bf16[576,128]{1,0:T(8,128)(2,1)S(1)} %get-tuple-element.14), channel_id=1, source_target_pairs={{0,1},{1,2},{2,3},{3,4},{4,5},{5,6},{6,7},{8,9},{9,10},{10,11},{11... | collective-permute-start | bytes 442376 | tf_op jit(solution)/shard_map/ppermute | solution.py:401
  82.6 6.5 %collective-permute-start.1 = (bf16[576,128]{1,0:T(8,128)(2,1)S(1)}, bf16[576,128]{1,0:T(8,128)(2,1)S(1)}, u32[]{:S(2)}, u32[]{:S(2)}) collective-permute-start(bf16[576,128]{1,0:T(8,128)(2,1)S(1)} %get-tuple-element.15), channel_id=1, source_target_pairs={{1,0},{2,1},{3,2},{4,3},{5,4},{6,5},{7,6},{9,8},{10,9},{11,10},{12... | collective-permute-start | bytes 442376 | tf_op jit(solution)/shard_map/ppermute | solution.py:401
  89.1 5.9 %collective-permute-start.2 = (bf16[4,128,128]{2,1,0:T(8,128)(2,1)S(1)}, bf16[4,128,128]{2,1,0:T(8,128)(2,1)S(1)}, u32[]{:S(2)}, u32[]{:S(2)}) collective-permute-start(bf16[4,128,128]{2,1,0:T(8,128)(2,1)S(1)} %get-tuple-element.18), channel_id=1, source_target_pairs={{0,8},{8,16},{16,24},{24,32},{32,40},{40,48},{48,56},{56,64},{64,7... | collective-permute-start | bytes 393224 | tf_op jit(solution)/shard_map/ppermute | solution.py:401
  90.4 5.7 %collective-permute-start.3 = (bf16[4,128,128]{2,1,0:T(8,128)(2,1)S(1)}, bf16[4,128,128]{2,1,0:T(8,128)(2,1)S(1)}, u32[]{:S(2)}, u32[]{:S(2)}) collective-permute-start(bf16[4,128,128]{2,1,0:T(8,128)(2,1)S(1)} %get-tuple-element.19), channel_id=1, source_target_pairs={{8,0},{16,8},{24,16},{32,24},{40,32},{48,40},{56,48},{64,56},{72,6... | collective-permute-start | bytes 393224 | tf_op jit(solution)/shard_map/ppermute | solution.py:401
